TPU v7x, 32 devices: a whole 2x2x4 slice. The times are simulated.
32 devices in a mesh: groups: 2 (over x), frame: 16 (over z, y, core).
Axes of the slice: x: 2, y: 2, z: 4, core: 2. Of those that a mesh axis runs over, the one named last changes fastest.
Arguments:
- frames_in: bfloat16 [32, 256, 2240], P(('groups', 'frame')), parts along dimension 0, may hold values from -16 to 16
- qkv_weight: bfloat16 [3, 2240, 1280], P(None, None, 'frame'), may hold values from -0.125 to 0.125
Outputs:
- attended: bfloat16 [32, 256, 1280], P(('groups', 'frame')), parts along dimension 0
There are 2 independent parts, one for each index of `groups`. A program takes and returns all parts, laid end to end along the dimension named above; an argument that names none is the same for every part. Nothing has to cross between parts.
All inputs are finite; a program needn't handle non-finite values.
Results may differ from a plain program's by a relative error of at most 0.0039.
Values may be sent and summed in bfloat16 or wider, within the bound.
A program may use at most 128 MiB of HBM per device.

v0:
```python
import jax
import jax.numpy as jnp
from jax import lax
from jax.sharding import PartitionSpec as P

HEAD_DIM = 32
HEADS = 40


EPSILON = 1e-06


def entering(shard, axis, join, neutral):
    place = lax.axis_index(axis)
    gathered = jax.tree.map(
        lambda a, kind: lax.all_gather(a.astype(kind), axis), shard, (jnp.bfloat16, jnp.bfloat16)
    )
    state = jax.tree.map(lambda a, e: jnp.zeros_like(a) + jnp.asarray(e, a.dtype), shard, neutral)

    def one(hop, state):
        return join(
            state,
            jax.tree.map(
                lambda a, own: lax.dynamic_index_in_dim(a, hop, 0, False).astype(own.dtype),
                gathered,
                shard,
            ),
        )

    return lax.fori_loop(0, place, one, state)


def add_pair(earlier, later):
    return (earlier[0] + later[0], earlier[1] + later[1])


def carry_states(key_rows, value_rows):
    count = key_rows.shape[0]
    feature_k = jax.nn.relu(key_rows).reshape(count, HEADS, HEAD_DIM)
    values = value_rows.reshape(count, HEADS, HEAD_DIM)
    local_state = jnp.einsum("thi,thj->hij", feature_k, values, preferred_element_type=jnp.float32)
    local_keys = jnp.sum(feature_k.astype(jnp.float32), axis=0)
    prior_state, prior_keys = entering(
        (local_state, local_keys),
        "frame",
        add_pair,
        (jnp.zeros_like(local_state), jnp.zeros_like(local_keys)),
    )
    return (local_state, local_keys, prior_state, prior_keys)


def apply_state(feature_q, state, key_sum):
    numer = jnp.einsum("thi,hij->thj", feature_q, state, precision=lax.Precision.HIGHEST)
    denom = jnp.einsum("thi,hi->th", feature_q, key_sum, precision=lax.Precision.HIGHEST)
    return (numer, denom)


def shards(frames_in, qkv_weight):
    tokens = frames_in[0]
    count = tokens.shape[0]
    weights_all = lax.all_gather(qkv_weight, "frame", axis=2, tiled=True)
    projected = jnp.einsum("td,sdc->stc", tokens, weights_all, preferred_element_type=jnp.float32)
    queries = projected[0]
    key_rows = projected[1].astype(jnp.bfloat16)
    value_rows = projected[2].astype(jnp.bfloat16)
    local_state, local_keys, prior_state, prior_keys = carry_states(key_rows, value_rows)
    feature_q = jax.nn.relu(queries).reshape(count, HEADS, HEAD_DIM)
    own_numer, own_denom = apply_state(feature_q, local_state, local_keys)
    past_numer, past_denom = apply_state(feature_q, prior_state, prior_keys)
    numer = past_numer + own_numer
    denom = past_denom + own_denom
    attended = (numer / (denom[:, :, None] + EPSILON)).astype(jnp.bfloat16)
    return attended.reshape(1, count, HEADS * HEAD_DIM)


def solution(mesh):
    placed = (P(("groups", "frame"), None, None), P(None, None, "frame"))
    return jax.shard_map(
        shards,
        mesh=mesh,
        in_specs=placed,
        out_specs=P(("groups", "frame"), None, None),
        check_vma=False,
    )
```

profile of v0, /device:TPU:26, one launch (start us, length us, event | category | flops | bytes accessed | tf_op | source)
XLA Modules:
  0.0 195.4 jit_solution(12941034522131766999)
XLA Ops:
  6.5 0.0 copy-start
  6.5 0.0 all-gather.4.cloned.1.call-start
  6.5 0.7 all-gather.4.cloned.1.call-update
  7.3 0.0 all-gather.6.cloned.1.call-start
  7.3 96.0 %all-gather.4.cloned.1.call-done = bf16[3,2240,1280]{1,2,0:T(8,128)(2,1)} async-done(((bf16[3,2240,80]{1,2,0:T(8,128)(2,1)}), bf16[3,2240,1280]{1,2,0:T(8,128)(2,1)}) %all-gather.4.cloned.1.call-update) | async-done | bytes 17203216 | tf_op jit(solution)/shard_map/all_gather | solution.py:61
  103.3 0.0 copy-done
  103.3 8.5 %convolution_bitcast_fusion = f32[3,256,1280]{1,2,0:T(8,128)S(1)} fusion(bf16[3,2240,1280]{1,2,0:T(8,128)(2,1)} %all-gather.4.cloned.1.call-done, bf16[1,256,2240]{1,2,0:T(8,128)(2,1)S(1)} %copy-done), kind=kOutput, calls=%fused_computation.3 | convolution fusion | flops 4404019200 | bytes 22282240 | tf_op jit(solution)/shard_map/td,sdc->stc/dot_general | solution.py:62
  111.8 0.3 convert_reduce_fusion
  112.1 0.1 slice.21
  112.2 1.3 fusion.8
  113.5 0.0 all-gather.6.cloned.1.call-update
  113.5 0.1 reshape.41
  113.6 0.1 convert_element_type.51
  113.6 0.1 copy.9
  113.7 16.9 %all_gather.16 = bf16[16,40,32]{1,2,0:T(8,128)(2,1)S(1)} all-gather(bf16[1,40,32]{1,2,0:T(8,128)(2,1)S(1)} %copy.9), channel_id=1, replica_groups=mesh['groups'=2,'frame'=16] {'frame'}, dimensions={0}, use_global_device_ids=true | all-gather | bytes 43520 | tf_op jit(solution)/shard_map/all_gather | solution.py:16
  130.6 0.8 fusion.11
  131.4 37.1 %all-gather.6.cloned.1.call-done = bf16[640,32,32]{2,1,0:T(8,128)(2,1)} async-done(((bf16[40,32,32]{2,1,0:T(8,128)(2,1)}), bf16[640,32,32]{2,1,0:T(8,128)(2,1)}) %all-gather.6.cloned.1.call-update) | async-done | bytes 1310736 | tf_op jit(solution)/shard_map/all_gather | solution.py:16
  168.4 0.1 broadcast_in_dim.7
  168.5 15.4 %while.12 = (s32[]{:T(128)}, f32[40,32,32]{2,1,0:T(8,128)S(1)}, f32[40,32]{1,0:T(8,128)S(1)}, s32[]{:T(128)}, bf16[16,40,32,32]{3,2,1,0:T(8,128)(2,1)}, /*index=...) while((s32[]{:T(128)}, f32[40,32,32]{2,1,0:T(8,128)S(1)}, f32[40,32]{1,0:T(8,128)S(1)}, ...), condition=%wide.region_2.3_spmd, body=%wide.region_1.2_spmd.sunk | while | flops 84485 | bytes 432775 | solution.py:30
  168.6 1.1 convert_add_fusion.4
  169.7 0.1 copy.24
  169.8 1.1 convert_add_fusion.4
  171.0 0.1 copy.24
  171.1 1.1 convert_add_fusion.4
  172.3 0.1 copy.24
  172.4 1.1 convert_add_fusion.4
  173.5 0.1 copy.24
  173.7 1.1 convert_add_fusion.4
  174.8 0.1 copy.24
  175.0 1.1 convert_add_fusion.4
  176.1 0.1 copy.24
  176.2 1.1 convert_add_fusion.4
  177.4 0.1 copy.24
  177.5 1.1 convert_add_fusion.4
  178.7 0.1 copy.24
  178.8 1.1 convert_add_fusion.4
  179.9 0.1 copy.24
  180.1 1.1 convert_add_fusion.4
  181.2 0.1 copy.24
  181.4 1.1 convert_add_fusion.4
  182.5 0.1 copy.24
  182.6 1.1 convert_add_fusion.4
  183.8 0.1 copy.24
  183.9 0.8 fusion.10
  184.7 0.0 copy-start.1
  184.7 1.3 fusion.9
  186.0 0.0 copy-done.1
  186.0 1.4 fusion.2
  187.4 1.1 copy.13
  (27 shorter events, 0.2 us)
Async XLA Ops:
  6.5 96.8 %copy-start = (bf16[1,256,2240]{1,2,0:T(8,128)(2,1)S(1)}, bf16[1,256,2240]{1,2,0:T(8,128)(2,1)}, u32[]{:S(2)}) copy-start(bf16[1,256,2240]{1,2,0:T(8,128)(2,1)} %param.4) | copy-start | bytes 3440644
  6.5 96.8 %all-gather.4.cloned.1.call-start = ((), (), s32[]{:S(2)}) async-start(), calls=%async_computation | async-start | bytes 18800640 | tf_op jit(solution)/shard_map/all_gather | solution.py:61
  7.3 161.2 %all-gather.6.cloned.1.call-start = ((), (), s32[]{:S(2)}) async-start(), calls=%async_computation.1 | async-start | bytes 5570560 | tf_op jit(solution)/shard_map/all_gather | solution.py:16
  184.7 1.4 copy-start.1
Sparse Core Ops, SparseCore 0:
  8.9 94.3 all-gather.3
  113.6 54.8 all-gather.5
where the time goes:
time: 199 us; the launch traced here: 195 us
  waiting for transfers between devices  134 us (67%)
  blocking collectives  16.9 us (8%)
  matrix products  14 us (7%)
  other arithmetic  14 us (7%)
  between operations  13.5 us (7%)
  local copies, waits for them, and re-layouts  2.63 us (1%)
    all_gather x1, waiting for transfers between devices, shards(): weights_all = lax.all_gather(qkv_weight, 'frame', axis=2, tiled=True)  96 us
    all_gather x1, waiting for transfers between devices, entering(): lax.all_gather(a.astype(kind), axis)  37.1 us
    all_gather x1, blocking collectives, entering(): lax.all_gather(a.astype(kind), axis)  16.9 us
    add x24, other arithmetic, add_pair(): return (earlier[0] + later[0], earlier[1] + later[1])  13.7 us
    dot_general x1, matrix products, shards(): jnp.einsum('td,sdc->stc', tokens, weights_all, preferred_element_type=jnp...  8.52 us
  transfers between devices with their start and end apart: 2, of which 2 were waited for; matrix products, arithmetic and copies ran while one was open for 1% of the time, Pallas kernels for 0%

commit v1 on v0

--- a/solution.py
+++ b/solution.py
@@ -1,6 +1,10 @@
+import functools
+
 import jax
 import jax.numpy as jnp
 from jax import lax
+from jax.experimental import pallas as pl
+from jax.experimental.pallas import tpu as pltpu
 from jax.sharding import PartitionSpec as P
 
 HEAD_DIM = 32
@@ -55,7 +59,7 @@
     return (numer, denom)
 
 
-def shards(frames_in, qkv_weight):
+def gathered_shards(frames_in, qkv_weight):
     tokens = frames_in[0]
     count = tokens.shape[0]
     weights_all = lax.all_gather(qkv_weight, "frame", axis=2, tiled=True)
@@ -73,8 +77,313 @@
     return attended.reshape(1, count, HEADS * HEAD_DIM)
 
 
+K, V, Q = 0, 1, 2
+KIND_AT = (1, 2, 0)
+
+
+def kernel(
+    lines, x_in, w_in, out, wbuf, xbuf, obuf, st, sib, total, pre, chain,
+    w_recv, z_send, x_send, d_send, own_sem, fx_local, fx_send, fx_recv,
+    s_send, s_recv, c_send, c_recv, o_local, o_send, o_recv,
+):
+    half_rows = w_in.shape[1]
+    rows = 2 * half_rows
+    group_heads = rows // HEAD_DIM
+    bf16, f32 = jnp.bfloat16, jnp.float32
+
+    x = lax.axis_index("groups")
+    f = lax.axis_index("frame")
+    z, y, c = f // 4, (f // 2) % 2, f % 2
+    primary = c == x
+    first, last = z == 0, z == lines - 1
+
+    def place(x, z, y, c):
+        return {"groups": x, "frame": z * 4 + y * 2 + c}
+
+    left, right = place(x, z - 1, y, c), place(x, z + 1, y, c)
+    sibling, across, facing = place(x, z, y, 1 - c), place(1 - x, z, y, c), place(x, z, 1 - y, c)
+
+    inner = jnp.where((z == 0) | (z == lines - 1), 0, 1)
+    low = z < 2
+    order = [z]
+    for k in (1, 2, 3):
+        end = jnp.where(low, k, 3 - k)
+        mid = jnp.where(low, (1, 0, 2, 3)[k], (2, 3, 1, 0)[k])
+        order.append(jnp.where(inner == 1, mid, end))
+
+    def block(kind, g, h):
+        return wbuf.at[g, pl.ds(pl.multiple_of(kind * rows + h * half_rows, 16), half_rows), :]
+
+    def w_copy(src, kind, g, send, to):
+        return pltpu.make_async_remote_copy(
+            src_ref=src, dst_ref=block(kind, g, c), send_sem=send,
+            recv_sem=w_recv.at[kind, g, c], device_id=to, device_id_type=pl.DeviceIdType.MESH,
+        )
+
+    def w_arrived(kind, g, h):
+        pltpu.make_async_copy(block(kind, g, h), block(kind, g, h), w_recv.at[kind, g, h]).wait()
+
+    barrier = pltpu.get_barrier_semaphore()
+
+    def greet(who):
+        pl.semaphore_signal(barrier, inc=1, device_id=who, device_id_type=pl.DeviceIdType.MESH)
+
+    greet(sibling)
+    greet(across)
+    greet(facing)
+
+    @pl.when(jnp.logical_not(first))
+    def _():
+        greet(left)
+
+    @pl.when(jnp.logical_not(last))
+    def _():
+        greet(right)
+
+    own_copies = [
+        pltpu.make_async_copy(w_in.at[KIND_AT[kind]], block(kind, z, c), own_sem.at[kind])
+        for kind in (K, V, Q)
+    ]
+    frame_local = pltpu.make_async_copy(x_in, xbuf.at[y], fx_local)
+    frame_local.start()
+    for copy in own_copies:
+        copy.start()
+
+    pl.semaphore_wait(barrier, 3 + jnp.where(first, 0, 1) + jnp.where(last, 0, 1))
+
+    def own_z(kind, op):
+        src = w_in.at[KIND_AT[kind]]
+
+        @pl.when(primary & jnp.logical_not(first))
+        def _():
+            op(w_copy(src, kind, z, z_send.at[0, kind, z], left))
+
+        @pl.when(primary & jnp.logical_not(last))
+        def _():
+            op(w_copy(src, kind, z, z_send.at[1, kind, z], right))
+
+    def own_d(kind):
+        return w_copy(w_in.at[KIND_AT[kind]], kind, z, d_send.at[kind, z], sibling)
+
+    def forward(kind, g, op):
+        src = block(kind, g, c)
+
+        @pl.when(primary & (g > z) & jnp.logical_not(first))
+        def _():
+            op(w_copy(src, kind, g, z_send.at[0, kind, g], left))
+
+        @pl.when(primary & (g < z) & jnp.logical_not(last))
+        def _():
+            op(w_copy(src, kind, g, z_send.at[1, kind, g], right))
+
+        @pl.when(primary)
+        def _():
+            op(w_copy(src, kind, g, x_send.at[kind, g], across))
+
+        op(w_copy(src, kind, g, d_send.at[kind, g], sibling))
+
+    start = lambda copy: copy.start()
+    sent = lambda copy: copy.wait_send()
+
+    own_z(K, start)
+    own_z(V, start)
+    frame_far = pltpu.make_async_remote_copy(
+        src_ref=x_in, dst_ref=xbuf.at[y], send_sem=fx_send, recv_sem=fx_recv,
+        device_id=facing, device_id_type=pl.DeviceIdType.MESH,
+    )
+    frame_far.start()
+    for kind in (K, V, Q):
+        own_d(kind).start()
+
+    def relay(kind, g):
+        w_arrived(kind, g, c)
+        forward(kind, g, start)
+
+    row_head = lax.broadcasted_iota(jnp.int32, (rows, rows), 0) // HEAD_DIM
+    col_head = lax.broadcasted_iota(jnp.int32, (rows, rows), 1) // HEAD_DIM
+    same_head = row_head == col_head
+
+    def states(g, side):
+        kv = jnp.dot(wbuf[g, 0 : 2 * rows, :], xbuf[side], preferred_element_type=f32)
+        keys = jnp.maximum(kv[:rows].astype(bf16), jnp.zeros((), bf16))
+        values = kv[rows:].astype(bf16)
+        values = jnp.concatenate([values, jnp.ones((16, values.shape[1]), bf16)], axis=0)
+        full = lax.dot_general(values, keys, (((1,), (1,)), ((), ())), preferred_element_type=f32)
+        kept = jnp.where(same_head, full[:rows], 0.0)
+        packed = kept[0:HEAD_DIM]
+        for h in range(1, group_heads):
+            packed = packed + kept[h * HEAD_DIM : (h + 1) * HEAD_DIM]
+        st[side, g, 0:HEAD_DIM, :] = packed
+        st[side, g, HEAD_DIM : HEAD_DIM + 8, :] = full[rows : rows + 8]
+
+    def attend(g, side):
+        queries = jnp.dot(wbuf[g, 2 * rows : 3 * rows, :], xbuf[side], preferred_element_type=f32)
+        queries = jnp.maximum(queries, 0.0)
+        q_hi = queries.astype(bf16)
+        q_lo = (queries - q_hi.astype(f32)).astype(bf16)
+        packed = total[side, g]
+        numer = jnp.concatenate([packed[0:HEAD_DIM]] * group_heads, axis=0)
+        denom = jnp.concatenate([packed[HEAD_DIM : HEAD_DIM + 8]] * (rows // 8), axis=0)
+        state = jnp.concatenate(
+            [jnp.where(same_head, numer, 0.0), jnp.where(same_head, denom, 0.0)], axis=0
+        )
+        s_hi = state.astype(bf16)
+        s_lo = (state - s_hi.astype(f32)).astype(bf16)
+        both = (
+            jnp.dot(s_hi, q_hi, preferred_element_type=f32)
+            + jnp.dot(s_hi, q_lo, preferred_element_type=f32)
+            + jnp.dot(s_lo, q_hi, preferred_element_type=f32)
+        )
+        obuf[side, g] = (both[:rows] / (both[rows:] + EPSILON)).astype(bf16)
+
+    def out_rows(g):
+        return out.at[pl.ds(pl.multiple_of((2 * g + y) * rows, 16), rows), :]
+
+    def out_local(g):
+        return pltpu.make_async_copy(obuf.at[y, g], out_rows(g), o_local.at[g])
+
+    def out_far(g):
+        return pltpu.make_async_remote_copy(
+            src_ref=obuf.at[1 - y, g], dst_ref=out_rows(g), send_sem=o_send.at[g],
+            recv_sem=o_recv.at[g], device_id=facing, device_id_type=pl.DeviceIdType.MESH,
+        )
+
+    frame_local.wait()
+    for copy in own_copies:
+        copy.wait()
+
+    for k in (1, 2, 3):
+        for kind in (K, V):
+            relay(kind, order[k])
+        for kind in (K, V):
+            w_arrived(kind, order[k - 1], 1 - c)
+        states(order[k - 1], y)
+    own_z(Q, start)
+    for kind in (K, V):
+        w_arrived(kind, order[3], 1 - c)
+    states(order[3], y)
+    frame_far.wait_recv()
+
+    @pl.loop(0, 2)
+    def _(g):
+        states(g, 1 - y)
+
+    relay(Q, order[1])
+
+    @pl.loop(2, 4)
+    def _(g):
+        states(g, 1 - y)
+
+    swap = pltpu.make_async_remote_copy(
+        src_ref=st, dst_ref=sib, send_sem=s_send, recv_sem=s_recv,
+        device_id=sibling, device_id_type=pl.DeviceIdType.MESH,
+    )
+    swap.start()
+    swap.wait_recv()
+    near = st[0] + sib[0]
+    whole = near + st[1] + sib[1]
+    later = jnp.where(c == 1, 1.0, 0.0).astype(f32)
+
+    def onward():
+        return pltpu.make_async_remote_copy(
+            src_ref=chain, dst_ref=pre, send_sem=c_send, recv_sem=c_recv,
+            device_id=right, device_id_type=pl.DeviceIdType.MESH,
+        )
+
+    @pl.when(first)
+    def _():
+        pre[...] = jnp.zeros_like(pre)
+
+    @pl.when(jnp.logical_not(first))
+    def _():
+        pltpu.make_async_copy(pre, pre, c_recv).wait()
+
+    @pl.when(jnp.logical_not(last))
+    def _():
+        chain[...] = pre[...] + whole
+        onward().start()
+
+    before = pre[...]
+    total[0] = before + st[0] + later * sib[0]
+    total[1] = before + near + st[1] + later * sib[1]
+
+    def finish(g):
+        w_arrived(Q, g, 1 - c)
+        attend(g, 1 - y)
+        out_far(g).start()
+        attend(g, y)
+        out_local(g).start()
+
+    relay(Q, order[2])
+    finish(order[0])
+    relay(Q, order[3])
+    for k in (1, 2, 3):
+        finish(order[k])
+
+    for kind in (K, V, Q):
+        own_z(kind, sent)
+        own_d(kind).wait_send()
+        for k in (1, 2, 3):
+            forward(kind, order[k], sent)
+    frame_far.wait_send()
+    swap.wait_send()
+
+    @pl.when(jnp.logical_not(last))
+    def _():
+        onward().wait_send()
+
+    for g in range(4):
+        out_local(g).wait()
+        out_far(g).wait_send()
+    for g in range(4):
+        theirs = out.at[pl.ds(pl.multiple_of((2 * g + 1 - y) * rows, 16), rows), :]
+        pltpu.make_async_copy(theirs, theirs, o_recv.at[g]).wait()
+
+
+def kernel_shards(lines, frames_in, qkv_weight):
+    tokens = jnp.swapaxes(frames_in[0], 0, 1)
+    weights = jnp.swapaxes(qkv_weight, 1, 2)
+    depth, count = tokens.shape
+    half_rows = weights.shape[1]
+    rows = 2 * half_rows
+    dma = pltpu.SemaphoreType.DMA
+    bf16, f32 = jnp.bfloat16, jnp.float32
+    packed = (lines, HEAD_DIM + 8, rows)
+    out = pl.pallas_call(
+        functools.partial(kernel, lines),
+        out_shape=jax.ShapeDtypeStruct((HEADS * HEAD_DIM, count), bf16),
+        in_specs=[pl.BlockSpec(memory_space=pl.ANY)] * 2,
+        out_specs=pl.BlockSpec(memory_space=pl.ANY),
+        scratch_shapes=[
+            pltpu.VMEM((lines, 3 * rows, depth), bf16),
+            pltpu.VMEM((2, depth, count), bf16),
+            pltpu.VMEM((2, lines, rows, count), bf16),
+            pltpu.VMEM((2,) + packed, f32),
+            pltpu.VMEM((2,) + packed, f32),
+            pltpu.VMEM((2,) + packed, f32),
+            pltpu.VMEM(packed, f32),
+            pltpu.VMEM(packed, f32),
+            dma((3, lines, 2)),
+            dma((2, 3, lines)),
+            dma((3, lines)),
+            dma((3, lines)),
+            dma((3,)),
+            dma, dma, dma, dma, dma, dma, dma,
+            dma((lines,)),
+            dma((lines,)),
+            dma((lines,)),
+        ],
+        compiler_params=pltpu.CompilerParams(
+            collective_id=0, has_side_effects=True, vmem_limit_bytes=48 * 1024 * 1024
+        ),
+    )(tokens, weights)
+    return jnp.swapaxes(out, 0, 1)[None]
+
+
 def solution(mesh):
     placed = (P(("groups", "frame"), None, None), P(None, None, "frame"))
+    fits = mesh.shape["groups"] == 2 and mesh.shape["frame"] == 16
+    shards = functools.partial(kernel_shards, mesh.shape["frame"] // 4) if fits else gathered_shards
     return jax.shard_map(
         shards,
         mesh=mesh,

time: 199 us -> 89.9 us (0.45); the launches traced: 195 us -> 88.7 us
  waiting for transfers between devices: 134 us -> 0 us
  Pallas kernels: 0 us -> 85.1 us
  blocking collectives: 16.9 us -> 0 us
  matrix products: 14 us -> 0 us
  other arithmetic: 14 us -> 0 us
  between operations: 13.5 us -> 0.01 us
    all_gather x2 -> x0, waiting for transfers between devices: 133 us -> none  [the longest x1 96 us: shards(): weights_all = lax.all_gather(qkv_weight, 'frame', axis=2, tiled=True)]
    pallas_call x0 -> x1, Pallas kernels: none -> 85.1 us  [kernel_shards(): pl.pallas_call(functools.partial(kernel, lines), out_shape=jax.ShapeDtype...]
    all_gather x1 -> x0, blocking collectives: 16.9 us -> none  [entering(): lax.all_gather(a.astype(kind), axis)]
    dot_general x6 -> x0, matrix products: 14 us -> none  [the longest x1 8.52 us: shards(): jnp.einsum('td,sdc->stc', tokens, weights_all, preferred_element_type=jnp...]
    add x25 -> x0, other arithmetic: 13.7 us -> none  [the longest x24 13.7 us: add_pair(): return (earlier[0] + later[0], earlier[1] + later[1])]
    unnamed x4, local copies, waits for them, and re-layouts: 0.01 us -> 2.5 us
  transfers between devices with their start and end apart: 2 -> 0, of which waited for: 2 -> 0; matrix products, arithmetic and copies ran while one was open for 1% -> 0% of each run, Pallas kernels for 0% -> 0%
where the time goes in v1:
time: 89.9 us; the launch traced here: 88.7 us
  Pallas kernels  85.1 us (95%)
  local copies, waits for them, and re-layouts  3.58 us (4%)
    pallas_call x1, Pallas kernels, kernel_shards(): pl.pallas_call(functools.partial(kernel, lines), out_shape=jax.ShapeDtype...  85.1 us
    unnamed x4, local copies, waits for them, and re-layouts  2.5 us

profile of v1, /device:TPU:26, one launch (start us, length us, event | category | flops | bytes accessed | tf_op | source)
XLA Modules:
  0.0 88.7 jit_solution(16395724744949073204)
XLA Ops:
  0.0 0.0 copy-start
  0.0 1.3 %copy-done = bf16[1,256,2240]{1,2,0:T(8,128)(2,1)S(1)} copy-done((bf16[1,256,2240]{1,2,0:T(8,128)(2,1)S(1)}, bf16[1,256,2240]{1,2,0:T(8,128)(2,1)}, u32[]{:S(2)}) %copy-start) | copy-done | bytes 1146904
  1.3 0.0 copy-start.1
  1.3 1.2 %copy-done.1 = bf16[3,2240,80]{1,2,0:T(8,128)(2,1)S(1)} copy-done((bf16[3,2240,80]{1,2,0:T(8,128)(2,1)S(1)}, bf16[3,2240,80]{1,2,0:T(8,128)(2,1)}, u32[]{:S(2)}) %copy-start.1) | copy-done | bytes 1075224
  2.5 85.1 %shard_map.28 = bf16[1280,256]{1,0:T(8,128)(2,1)S(1)} custom-call(bf16[2240,256]{1,0:T(8,128)(2,1)S(1)} %bitcast.8, bf16[3,80,2240]{2,1,0:T(8,128)(2,1)S(1)} %bitcast.9), custom_call_target="tpu_custom_call" | custom-call | tf_op jit(solution)/shard_map/pallas_call | solution.py:352
  87.6 1.1 %copy.3 = bf16[1,256,1280]{2,1,0:T(8,128)(2,1)} copy(bf16[1,256,1280]{1,2,0:T(8,128)(2,1)S(1)} %bitcast.7) | data formatting | bytes 1310720 | tf_op jit(solution)/shard_map/broadcast_in_dim | solution.py:380
Async XLA Ops:
  0.0 1.3 %copy-start = (bf16[1,256,2240]{1,2,0:T(8,128)(2,1)S(1)}, bf16[1,256,2240]{1,2,0:T(8,128)(2,1)}, u32[]{:S(2)}) copy-start(bf16[1,256,2240]{1,2,0:T(8,128)(2,1)} %param.2) | copy-start | bytes 3440644
  1.3 1.2 %copy-start.1 = (bf16[3,2240,80]{1,2,0:T(8,128)(2,1)S(1)}, bf16[3,2240,80]{1,2,0:T(8,128)(2,1)}, u32[]{:S(2)}) copy-start(bf16[3,2240,80]{1,2,0:T(8,128)(2,1)} %param.3) | copy-start | bytes 3225604

commit v2 on v1

--- a/solution.py
+++ b/solution.py
@@ -82,9 +82,9 @@
 
 
 def kernel(
-    lines, x_in, w_in, out, wbuf, xbuf, obuf, st, sib, total, pre, chain,
+    lines, x_in, w_in, out, wbuf, xbuf, qbuf, obuf, st, sib, total, pre, chain,
     w_recv, z_send, x_send, d_send, own_sem, fx_local, fx_send, fx_recv,
-    s_send, s_recv, c_send, c_recv, o_local, o_send, o_recv,
+    s_send, s_recv, c_send, c_recv, h_send, h_recv, o_local, o_send, o_recv,
 ):
     half_rows = w_in.shape[1]
     rows = 2 * half_rows
@@ -216,9 +216,12 @@
         st[side, g, 0:HEAD_DIM, :] = packed
         st[side, g, HEAD_DIM : HEAD_DIM + 8, :] = full[rows : rows + 8]
 
+    def project(g, side):
+        queries = jnp.dot(wbuf[g, 2 * rows : 3 * rows, :], xbuf[side], preferred_element_type=f32)
+        qbuf[side, g] = jnp.maximum(queries, 0.0)
+
     def attend(g, side):
-        queries = jnp.dot(wbuf[g, 2 * rows : 3 * rows, :], xbuf[side], preferred_element_type=f32)
-        queries = jnp.maximum(queries, 0.0)
+        queries = qbuf[side, g]
         q_hi = queries.astype(bf16)
         q_lo = (queries - q_hi.astype(f32)).astype(bf16)
         packed = total[side, g]
@@ -262,15 +265,10 @@
     for kind in (K, V):
         w_arrived(kind, order[3], 1 - c)
     states(order[3], y)
+    relay(Q, order[1])
     frame_far.wait_recv()
 
-    @pl.loop(0, 2)
-    def _(g):
-        states(g, 1 - y)
-
-    relay(Q, order[1])
-
-    @pl.loop(2, 4)
+    @pl.loop(0, 4)
     def _(g):
         states(g, 1 - y)
 
@@ -279,46 +277,68 @@
         device_id=sibling, device_id_type=pl.DeviceIdType.MESH,
     )
     swap.start()
+    relay(Q, order[2])
+
+    mine = pl.ds(2 * c, 2)
+    onward = pltpu.make_async_remote_copy(
+        src_ref=chain.at[mine], dst_ref=pre.at[mine], send_sem=c_send, recv_sem=c_recv,
+        device_id=right, device_id_type=pl.DeviceIdType.MESH,
+    )
+    share = pltpu.make_async_remote_copy(
+        src_ref=pre.at[mine], dst_ref=pre.at[mine], send_sem=h_send, recv_sem=h_recv,
+        device_id=sibling, device_id_type=pl.DeviceIdType.MESH,
+    )
     swap.wait_recv()
     near = st[0] + sib[0]
-    whole = near + st[1] + sib[1]
     later = jnp.where(c == 1, 1.0, 0.0).astype(f32)
-
-    def onward():
-        return pltpu.make_async_remote_copy(
-            src_ref=chain, dst_ref=pre, send_sem=c_send, recv_sem=c_recv,
-            device_id=right, device_id_type=pl.DeviceIdType.MESH,
-        )
+    total[0] = st[0] + later * sib[0]
+    total[1] = near + st[1] + later * sib[1]
+    chain[...] = near + st[1] + sib[1]
 
     @pl.when(first)
     def _():
-        pre[...] = jnp.zeros_like(pre)
+        onward.start()
+
+    def project_both(g):
+        w_arrived(Q, g, 1 - c)
+
+        @pl.loop(0, 2)
+        def _(side):
+            project(g, side)
+
+    project_both(order[0])
+    relay(Q, order[3])
 
     @pl.when(jnp.logical_not(first))
     def _():
-        pltpu.make_async_copy(pre, pre, c_recv).wait()
-
-    @pl.when(jnp.logical_not(last))
-    def _():
-        chain[...] = pre[...] + whole
-        onward().start()
-
-    before = pre[...]
-    total[0] = before + st[0] + later * sib[0]
-    total[1] = before + near + st[1] + later * sib[1]
+        pltpu.make_async_copy(pre.at[mine], pre.at[mine], c_recv).wait()
+
+        @pl.when(jnp.logical_not(last))
+        def _():
+            chain[mine] = chain[mine] + pre[mine]
+            onward.start()
+
+        share.start()
+
+    for k in (1, 2):
+        project_both(order[k])
+
+    @pl.when(jnp.logical_not(first))
+    def _():
+        share.wait_recv()
+        total[0] = total[0] + pre[...]
+        total[1] = total[1] + pre[...]
 
     def finish(g):
-        w_arrived(Q, g, 1 - c)
         attend(g, 1 - y)
         out_far(g).start()
         attend(g, y)
         out_local(g).start()
 
-    relay(Q, order[2])
-    finish(order[0])
-    relay(Q, order[3])
-    for k in (1, 2, 3):
+    for k in (0, 1, 2):
         finish(order[k])
+    project_both(order[3])
+    finish(order[3])
 
     for kind in (K, V, Q):
         own_z(kind, sent)
@@ -328,9 +348,13 @@
     frame_far.wait_send()
     swap.wait_send()
 
+    @pl.when(jnp.logical_not(first))
+    def _():
+        share.wait_send()
+
     @pl.when(jnp.logical_not(last))
     def _():
-        onward().wait_send()
+        onward.wait_send()
 
     for g in range(4):
         out_local(g).wait()
@@ -357,6 +381,7 @@
         scratch_shapes=[
             pltpu.VMEM((lines, 3 * rows, depth), bf16),
             pltpu.VMEM((2, depth, count), bf16),
+            pltpu.VMEM((2, lines, rows, count), f32),
             pltpu.VMEM((2, lines, rows, count), bf16),
             pltpu.VMEM((2,) + packed, f32),
             pltpu.VMEM((2,) + packed, f32),
@@ -368,13 +393,13 @@
             dma((3, lines)),
             dma((3, lines)),
             dma((3,)),
-            dma, dma, dma, dma, dma, dma, dma,
+            dma, dma, dma, dma, dma, dma, dma, dma, dma,
             dma((lines,)),
             dma((lines,)),
             dma((lines,)),
         ],
         compiler_params=pltpu.CompilerParams(
-            collective_id=0, has_side_effects=True, vmem_limit_bytes=48 * 1024 * 1024
+            collective_id=0, has_side_effects=True, vmem_limit_bytes=63 * 1024 * 1024
         ),
     )(tokens, weights)
     return jnp.swapaxes(out, 0, 1)[None]

time: 89.9 us -> 77.9 us (0.87); the launches traced: 88.7 us -> 77.7 us
  Pallas kernels: 85.1 us -> 75.5 us
  local copies, waits for them, and re-layouts: 3.58 us -> 2.16 us
    pallas_call x1, Pallas kernels: 85.1 us -> 75.5 us  [kernel_shards(): pl.pallas_call(functools.partial(kernel, lines), out_shape=jax.ShapeDtype...]
    unnamed x4 -> x0, local copies, waits for them, and re-layouts: 2.5 us -> none
    broadcast_in_dim x1, local copies, waits for them, and re-layouts: 1.08 us -> 2.16 us  [kernel_shards(): return jnp.swapaxes(out, 0, 1)[None]]
where the time goes in v2:
time: 77.9 us; the launch traced here: 77.7 us
  Pallas kernels  75.5 us (97%)
  local copies, waits for them, and re-layouts  2.16 us (3%)
    pallas_call x1, Pallas kernels, kernel_shards(): pl.pallas_call(functools.partial(kernel, lines), out_shape=jax.ShapeDtype...  75.5 us
    broadcast_in_dim x1, local copies, waits for them, and re-layouts, kernel_shards(): return jnp.swapaxes(out, 0, 1)[None]  2.16 us

profile of v2, /device:TPU:26, one launch (start us, length us, event | category | flops | bytes accessed | tf_op | source)
XLA Modules:
  0.0 77.7 jit_solution(8635011890069579176)
XLA Ops:
  0.0 75.5 %shard_map.28 = bf16[1280,256]{1,0:T(8,128)(2,1)} custom-call(bf16[2240,256]{1,0:T(8,128)(2,1)} %bitcast.8, bf16[3,80,2240]{2,1,0:T(8,128)(2,1)} %bitcast.9), custom_call_target="tpu_custom_call" | custom-call | tf_op jit(solution)/shard_map/pallas_call | solution.py:376
  75.6 2.2 %copy.3 = bf16[1,256,1280]{2,1,0:T(8,128)(2,1)} copy(bf16[1,256,1280]{1,2,0:T(8,128)(2,1)} %bitcast.7) | data formatting | bytes 1310720 | tf_op jit(solution)/shard_map/broadcast_in_dim | solution.py:405

commit v3 on v2

--- a/solution.py
+++ b/solution.py
@@ -255,17 +255,31 @@
     for copy in own_copies:
         copy.wait()
 
+    def own_q(left_if, right_if):
+        src = w_in.at[KIND_AT[Q]]
+
+        @pl.when(primary & left_if)
+        def _():
+            w_copy(src, Q, z, z_send.at[0, Q, z], left).start()
+
+        @pl.when(primary & right_if)
+        def _():
+            w_copy(src, Q, z, z_send.at[1, Q, z], right).start()
+
     for k in (1, 2, 3):
         for kind in (K, V):
             relay(kind, order[k])
+        if k == 1:
+            own_q(z >= 2, z < 2)
+        if k == 3:
+            own_q(z == 1, z == 2)
+            relay(Q, order[1])
         for kind in (K, V):
             w_arrived(kind, order[k - 1], 1 - c)
         states(order[k - 1], y)
-    own_z(Q, start)
     for kind in (K, V):
         w_arrived(kind, order[3], 1 - c)
     states(order[3], y)
-    relay(Q, order[1])
     frame_far.wait_recv()
 
     @pl.loop(0, 4)
@@ -336,9 +350,14 @@
         out_local(g).start()
 
     for k in (0, 1, 2):
-        finish(order[k])
+        attend(order[k], 1 - y)
+        out_far(order[k]).start()
     project_both(order[3])
-    finish(order[3])
+    attend(order[3], 1 - y)
+    out_far(order[3]).start()
+    for k in range(4):
+        attend(order[k], y)
+        out_local(order[k]).start()
 
     for kind in (K, V, Q):
         own_z(kind, sent)

time: 77.9 us -> 73.7 us (0.946)
  Pallas kernels: 75.5 us -> 71.4 us
    pallas_call x1, Pallas kernels: 75.5 us -> 71.4 us  [kernel_shards(): pl.pallas_call(functools.partial(kernel, lines), out_shape=jax.ShapeDtype...]
where the time goes in v3:
time: 73.7 us; the launch traced here: 73.6 us
  Pallas kernels  71.4 us (97%)
  local copies, waits for them, and re-layouts  2.16 us (3%)
    pallas_call x1, Pallas kernels, kernel_shards(): pl.pallas_call(functools.partial(kernel, lines), out_shape=jax.ShapeDtype...  71.4 us
    broadcast_in_dim x1, local copies, waits for them, and re-layouts, kernel_shards(): return jnp.swapaxes(out, 0, 1)[None]  2.16 us

profile of v3, /device:TPU:26, one launch (start us, length us, event | category | flops | bytes accessed | tf_op | source)
XLA Modules:
  0.0 73.6 jit_solution(16085617304420766554)
XLA Ops:
  0.0 71.4 %shard_map.28 = bf16[1280,256]{1,0:T(8,128)(2,1)} custom-call(bf16[2240,256]{1,0:T(8,128)(2,1)} %bitcast.8, bf16[3,80,2240]{2,1,0:T(8,128)(2,1)} %bitcast.9), custom_call_target="tpu_custom_call" | custom-call | tf_op jit(solution)/shard_map/pallas_call | solution.py:395
  71.4 2.2 %copy.3 = bf16[1,256,1280]{2,1,0:T(8,128)(2,1)} copy(bf16[1,256,1280]{1,2,0:T(8,128)(2,1)} %bitcast.7) | data formatting | bytes 1310720 | tf_op jit(solution)/shard_map/broadcast_in_dim | solution.py:424
